TPU v7x, 512 devices: a whole 4x8x8 slice. The times are simulated.
512 devices in a mesh: dp: 32 (over y, z_hi, core), tensor: 16 (over z_lo, x).
Axes of the slice: x: 4, y: 8, z: 8 (z_hi: 2, z_lo: 4; z = z_hi * 4 + z_lo), core: 2. Of those that a mesh axis runs over, the one named last changes fastest.
Arguments:
- text_feats: bfloat16 [16384, 1152], P('dp', 'tensor'), may hold values from -4 to 4
- image_feats: bfloat16 [16384, 1152], P('dp', 'tensor'), may hold values from -4 to 4
- group_ids: int32 [16384], replicated, may hold values from 0 to 8191
- log_scale: float32 [1], replicated, may hold values from 4.5 to 4.8
- bias: float32 [1], replicated, may hold values from -13 to -11
Outputs:
- text_grad: float32 [16384, 1152], P('dp', 'tensor')
- image_grad: float32 [16384, 1152], P(('dp', 'tensor'))
All inputs are finite; a program needn't handle non-finite values.
Results may differ from a plain program's by a relative error of at most 0.0041.
Values may be sent and summed in bfloat16 or wider, within the bound.
A program may use at most 64 MiB of HBM per device.

v0:
```python
import jax
import jax.numpy as jnp
from jax import lax
from jax.sharding import PartitionSpec as P

D = 1152


def from_behind(block, axis, distance):
    devices = range(lax.axis_size(axis))
    route = [((i - distance) % len(devices), i) for i in devices]
    return lax.ppermute(block, axis, route)


def normalize(rows):
    wide = rows.astype(jnp.float32)
    inverse = lax.rsqrt(jnp.sum(wide * wide, axis=1, keepdims=True) + 1e-06)
    return (wide * inverse, inverse)


def unit_back(grad_hat, unit, inverse):
    return (grad_hat - unit * jnp.sum(unit * grad_hat, axis=1, keepdims=True)) * inverse


def tile_terms(piece, piece_groups, text_hat, text_groups, scale, offset):
    logits = (
        scale
        * lax.dot_general(
            piece, text_hat, (((1,), (1,)), ((), ())), preferred_element_type=jnp.float32
        )
        + offset
    )
    sign = jnp.where(
        piece_groups[:, None] == text_groups[None, :], jnp.float32(1.0), jnp.float32(-1.0)
    )
    slope = (-sign * jax.nn.sigmoid(-sign * logits)).astype(jnp.bfloat16)
    push = scale * jnp.dot(slope, text_hat, preferred_element_type=jnp.float32)
    return (slope, push)


def body(text_feats, image_feats, group_ids, log_scale, bias):
    scale = jnp.exp(log_scale[0])
    offset = bias[0]
    text_rows = lax.all_gather(text_feats, "tensor", axis=1, tiled=True)
    image_rows = lax.all_to_all(image_feats, "tensor", split_axis=0, concat_axis=1, tiled=True)
    text_unit, text_inverse = normalize(text_rows)
    image_unit, image_inverse = normalize(image_rows)
    text_hat = text_unit.astype(jnp.bfloat16)
    image_hat = image_unit.astype(jnp.bfloat16)
    count = text_rows.shape[0]
    width = image_rows.shape[0]
    n_cycle = lax.axis_size("dp")
    cycle_pos = lax.axis_index("dp")
    tensor_pos = lax.axis_index("tensor")
    text_groups = lax.dynamic_slice_in_dim(group_ids, cycle_pos * count, count, 0)

    def groups_of(anchor, length):
        return lax.dynamic_slice_in_dim(group_ids, anchor * count + tensor_pos * width, length, 0)

    slopes = jnp.zeros((n_cycle, width, count), jnp.bfloat16)
    seen = jnp.zeros((n_cycle, width, D), jnp.bfloat16)

    def step(turn, carry):
        piece, pushed, slopes, seen = carry
        anchor = (cycle_pos - turn) % n_cycle
        slope, push = tile_terms(
            piece, groups_of(anchor, width), text_hat, text_groups, scale, offset
        )
        slopes = lax.dynamic_update_index_in_dim(slopes, slope, turn, 0)
        seen = lax.dynamic_update_index_in_dim(seen, piece, turn, 0)
        pushed = pushed + push
        piece = from_behind(piece, "dp", 1)
        pushed = from_behind(pushed, "dp", 1)
        return (piece, pushed, slopes, seen)

    start_carry = (image_hat, jnp.zeros((width, D), jnp.float32), slopes, seen)
    _, pushed, slopes, seen = lax.fori_loop(0, n_cycle, step, start_carry)
    image_grad = unit_back(pushed, image_unit, image_inverse)
    flat_slopes = slopes.reshape(n_cycle * width, count)
    flat_seen = seen.reshape(n_cycle * width, D)
    text_push = scale * lax.dot_general(
        flat_slopes, flat_seen, (((0,), (0,)), ((), ())), preferred_element_type=jnp.float32
    )
    term = unit_back(text_push, text_unit, text_inverse)
    text_grad = lax.psum_scatter(term, "tensor", scatter_dimension=1, tiled=True)
    return (text_grad, image_grad)


def solution(mesh):
    placed = (P("dp", "tensor"), P("dp", "tensor"), P(), P(), P())
    return jax.shard_map(
        body,
        mesh=mesh,
        in_specs=placed,
        out_specs=(P("dp", "tensor"), P(("dp", "tensor"), None)),
        check_vma=False,
    )
```

profile of v0, /device:TPU:6, one launch (start us, length us, event | category | flops | bytes accessed | tf_op | source)
XLA Modules:
  0.0 754.2 jit_solution(10587062712460620080)
XLA Ops:
  9.5 10.2 %all-to-all-start = ((bf16[16,32,72]{2,1,0:T(8,128)(2,1)}), bf16[16,32,72]{2,1,0:T(8,128)(2,1)S(1)}, u32[]{:S(2)}, u32[]{:S(2)}) async-start(bf16[16,32,72]{2,1,0:T(8,128)(2,1)} %bitcast.3), calls=%async_computation | async-start | bytes 262144 | tf_op jit(solution)/shard_map/all_to_all | solution.py:45
  26.9 67.8 %all-gather.2.cloned.1.call-done = bf16[512,1152]{0,1:T(8,128)(2,1)} async-done(((bf16[512,72]{0,1:T(8,128)(2,1)}), bf16[512,1152]{0,1:T(8,128)(2,1)}) %all-gather.2.cloned.1.call-update) | async-done | bytes 1179664 | tf_op jit(solution)/shard_map/all_gather | solution.py:44
  97.0 553.0 %while.21 = (s32[]{:T(128)}, bf16[32,1152]{1,0:T(8,128)(2,1)S(1)}, f32[32,1152]{1,0:T(8,128)S(1)}, bf16[32,32,512]{2,1,0:T(8,128)(2,1)}, bf16[32,32,1152]{2,1,0:...) while((s32[]{:T(128)}, bf16[32,1152]{1,0:T(8,128)(2,1)S(1)}, ...), condition=%wide.region_3.4_spmd, body=%wide.region_2.3_spmd.sunk | while | flops 75751440 | bytes 4010800 | solution.py:77
  108.7 5.9 collective-permute-done.1
  160.8 5.6 collective-permute-done.1
  178.1 5.7 collective-permute-done.1
  195.4 5.9 collective-permute-done.1
  213.0 5.6 collective-permute-done.1
  230.2 5.6 collective-permute-done.1
  299.2 5.6 collective-permute-done.1
  316.5 5.6 collective-permute-done.1
  333.8 5.6 collective-permute-done.1
  351.0 5.6 collective-permute-done.1
  368.3 5.6 collective-permute-done.1
  437.3 5.6 collective-permute-done.1
  471.8 5.6 collective-permute-done.1
  489.1 5.6 collective-permute-done.1
  540.8 5.6 collective-permute-done.1
  558.1 5.6 collective-permute-done.1
  592.6 5.6 collective-permute-done.1
  609.9 5.6 collective-permute-done.1
  627.1 5.6 collective-permute-done.1
  644.4 5.6 collective-permute-done.1
  658.2 89.1 %reduce-scatter.4.cloned.1.call-done = f32[72,512]{1,0:T(8,128)} async-done(((f32[1152,512]{1,0:T(8,128)}), f32[72,512]{1,0:T(8,128)}) %reduce-scatter.4.cloned.1.call-update) | async-done | bytes 147472
  (301 shorter events, 458.5 us)
Async XLA Ops:
  7.2 87.5 %all-gather.2.cloned.1.call-start = ((), (), s32[]{:S(2)}) async-start(), calls=%async_computation.2 | async-start | bytes 1253376 | tf_op jit(solution)/shard_map/all_gather | solution.py:44
  9.5 16.3 %all-to-all-start = ((bf16[16,32,72]{2,1,0:T(8,128)(2,1)}), bf16[16,32,72]{2,1,0:T(8,128)(2,1)S(1)}, u32[]{:S(2)}, u32[]{:S(2)}) async-start(bf16[16,32,72]{2,1,0:T(8,128)(2,1)} %bitcast.3), calls=%async_computation | async-start | bytes 262144 | tf_op jit(solution)/shard_map/all_to_all | solution.py:45
  19.8 727.6 %reduce-scatter.4.cloned.1.call-start = ((), (), s32[]{:S(2)}) async-start(), calls=%async_computation.3 | async-start | bytes 2506752
  101.8 12.8 %collective-permute-start.1 = (f32[32,1152]{1,0:T(8,128)S(1)}, f32[32,1152]{1,0:T(8,128)S(1)}, u32[]{:S(2)}, u32[]{:S(2)}) collective-permute-start(f32[32,1152]{1,0:T(8,128)S(1)} %fusion.33), channel_id=1, source_target_pairs={{496,0},{0,16},{16,32},{32,48},{48,64},{64,80},{80,96},{96,112},{1... | collective-permute-start | bytes 442376 | tf_op jit(solution)/shard_map/while/body/eval_jaxpr/ppermute | solution.py:12
  119.4 12.5 %collective-permute-start.1 = (f32[32,1152]{1,0:T(8,128)S(1)}, f32[32,1152]{1,0:T(8,128)S(1)}, u32[]{:S(2)}, u32[]{:S(2)}) collective-permute-start(f32[32,1152]{1,0:T(8,128)S(1)} %fusion.33), channel_id=1, source_target_pairs={{496,0},{0,16},{16,32},{32,48},{48,64},{64,80},{80,96},{96,112},{1... | collective-permute-start | bytes 442376 | tf_op jit(solution)/shard_map/while/body/eval_jaxpr/ppermute | solution.py:12
  136.7 12.5 %collective-permute-start.1 = (f32[32,1152]{1,0:T(8,128)S(1)}, f32[32,1152]{1,0:T(8,128)S(1)}, u32[]{:S(2)}, u32[]{:S(2)}) collective-permute-start(f32[32,1152]{1,0:T(8,128)S(1)} %fusion.33), channel_id=1, source_target_pairs={{496,0},{0,16},{16,32},{32,48},{48,64},{64,80},{80,96},{96,112},{1... | collective-permute-start | bytes 442376 | tf_op jit(solution)/shard_map/while/body/eval_jaxpr/ppermute | solution.py:12
  153.9 12.5 %collective-permute-start.1 = (f32[32,1152]{1,0:T(8,128)S(1)}, f32[32,1152]{1,0:T(8,128)S(1)}, u32[]{:S(2)}, u32[]{:S(2)}) collective-permute-start(f32[32,1152]{1,0:T(8,128)S(1)} %fusion.33), channel_id=1, source_target_pairs={{496,0},{0,16},{16,32},{32,48},{48,64},{64,80},{80,96},{96,112},{1... | collective-permute-start | bytes 442376 | tf_op jit(solution)/shard_map/while/body/eval_jaxpr/ppermute | solution.py:12
  171.2 12.5 %collective-permute-start.1 = (f32[32,1152]{1,0:T(8,128)S(1)}, f32[32,1152]{1,0:T(8,128)S(1)}, u32[]{:S(2)}, u32[]{:S(2)}) collective-permute-start(f32[32,1152]{1,0:T(8,128)S(1)} %fusion.33), channel_id=1, source_target_pairs={{496,0},{0,16},{16,32},{32,48},{48,64},{64,80},{80,96},{96,112},{1... | collective-permute-start | bytes 442376 | tf_op jit(solution)/shard_map/while/body/eval_jaxpr/ppermute | solution.py:12
  188.5 12.8 %collective-permute-start.1 = (f32[32,1152]{1,0:T(8,128)S(1)}, f32[32,1152]{1,0:T(8,128)S(1)}, u32[]{:S(2)}, u32[]{:S(2)}) collective-permute-start(f32[32,1152]{1,0:T(8,128)S(1)} %fusion.33), channel_id=1, source_target_pairs={{496,0},{0,16},{16,32},{32,48},{48,64},{64,80},{80,96},{96,112},{1... | collective-permute-start | bytes 442376 | tf_op jit(solution)/shard_map/while/body/eval_jaxpr/ppermute | solution.py:12
  206.1 12.5 %collective-permute-start.1 = (f32[32,1152]{1,0:T(8,128)S(1)}, f32[32,1152]{1,0:T(8,128)S(1)}, u32[]{:S(2)}, u32[]{:S(2)}) collective-permute-start(f32[32,1152]{1,0:T(8,128)S(1)} %fusion.33), channel_id=1, source_target_pairs={{496,0},{0,16},{16,32},{32,48},{48,64},{64,80},{80,96},{96,112},{1... | collective-permute-start | bytes 442376 | tf_op jit(solution)/shard_map/while/body/eval_jaxpr/ppermute | solution.py:12
  223.3 12.5 %collective-permute-start.1 = (f32[32,1152]{1,0:T(8,128)S(1)}, f32[32,1152]{1,0:T(8,128)S(1)}, u32[]{:S(2)}, u32[]{:S(2)}) collective-permute-start(f32[32,1152]{1,0:T(8,128)S(1)} %fusion.33), channel_id=1, source_target_pairs={{496,0},{0,16},{16,32},{32,48},{48,64},{64,80},{80,96},{96,112},{1... | collective-permute-start | bytes 442376 | tf_op jit(solution)/shard_map/while/body/eval_jaxpr/ppermute | solution.py:12
  240.6 12.5 %collective-permute-start.1 = (f32[32,1152]{1,0:T(8,128)S(1)}, f32[32,1152]{1,0:T(8,128)S(1)}, u32[]{:S(2)}, u32[]{:S(2)}) collective-permute-start(f32[32,1152]{1,0:T(8,128)S(1)} %fusion.33), channel_id=1, source_target_pairs={{496,0},{0,16},{16,32},{32,48},{48,64},{64,80},{80,96},{96,112},{1... | collective-permute-start | bytes 442376 | tf_op jit(solution)/shard_map/while/body/eval_jaxpr/ppermute | solution.py:12
  257.8 12.5 %collective-permute-start.1 = (f32[32,1152]{1,0:T(8,128)S(1)}, f32[32,1152]{1,0:T(8,128)S(1)}, u32[]{:S(2)}, u32[]{:S(2)}) collective-permute-start(f32[32,1152]{1,0:T(8,128)S(1)} %fusion.33), channel_id=1, source_target_pairs={{496,0},{0,16},{16,32},{32,48},{48,64},{64,80},{80,96},{96,112},{1... | collective-permute-start | bytes 442376 | tf_op jit(solution)/shard_map/while/body/eval_jaxpr/ppermute | solution.py:12
  309.6 12.5 %collective-permute-start.1 = (f32[32,1152]{1,0:T(8,128)S(1)}, f32[32,1152]{1,0:T(8,128)S(1)}, u32[]{:S(2)}, u32[]{:S(2)}) collective-permute-start(f32[32,1152]{1,0:T(8,128)S(1)} %fusion.33), channel_id=1, source_target_pairs={{496,0},{0,16},{16,32},{32,48},{48,64},{64,80},{80,96},{96,112},{1... | collective-permute-start | bytes 442376 | tf_op jit(solution)/shard_map/while/body/eval_jaxpr/ppermute | solution.py:12
  326.9 12.5 %collective-permute-start.1 = (f32[32,1152]{1,0:T(8,128)S(1)}, f32[32,1152]{1,0:T(8,128)S(1)}, u32[]{:S(2)}, u32[]{:S(2)}) collective-permute-start(f32[32,1152]{1,0:T(8,128)S(1)} %fusion.33), channel_id=1, source_target_pairs={{496,0},{0,16},{16,32},{32,48},{48,64},{64,80},{80,96},{96,112},{1... | collective-permute-start | bytes 442376 | tf_op jit(solution)/shard_map/while/body/eval_jaxpr/ppermute | solution.py:12
  344.1 12.5 %collective-permute-start.1 = (f32[32,1152]{1,0:T(8,128)S(1)}, f32[32,1152]{1,0:T(8,128)S(1)}, u32[]{:S(2)}, u32[]{:S(2)}) collective-permute-start(f32[32,1152]{1,0:T(8,128)S(1)} %fusion.33), channel_id=1, source_target_pairs={{496,0},{0,16},{16,32},{32,48},{48,64},{64,80},{80,96},{96,112},{1... | collective-permute-start | bytes 442376 | tf_op jit(solution)/shard_map/while/body/eval_jaxpr/ppermute | solution.py:12
  395.9 12.5 %collective-permute-start.1 = (f32[32,1152]{1,0:T(8,128)S(1)}, f32[32,1152]{1,0:T(8,128)S(1)}, u32[]{:S(2)}, u32[]{:S(2)}) collective-permute-start(f32[32,1152]{1,0:T(8,128)S(1)} %fusion.33), channel_id=1, source_target_pairs={{496,0},{0,16},{16,32},{32,48},{48,64},{64,80},{80,96},{96,112},{1... | collective-permute-start | bytes 442376 | tf_op jit(solution)/shard_map/while/body/eval_jaxpr/ppermute | solution.py:12
  413.1 12.5 %collective-permute-start.1 = (f32[32,1152]{1,0:T(8,128)S(1)}, f32[32,1152]{1,0:T(8,128)S(1)}, u32[]{:S(2)}, u32[]{:S(2)}) collective-permute-start(f32[32,1152]{1,0:T(8,128)S(1)} %fusion.33), channel_id=1, source_target_pairs={{496,0},{0,16},{16,32},{32,48},{48,64},{64,80},{80,96},{96,112},{1... | collective-permute-start | bytes 442376 | tf_op jit(solution)/shard_map/while/body/eval_jaxpr/ppermute | solution.py:12
  430.4 12.5 %collective-permute-start.1 = (f32[32,1152]{1,0:T(8,128)S(1)}, f32[32,1152]{1,0:T(8,128)S(1)}, u32[]{:S(2)}, u32[]{:S(2)}) collective-permute-start(f32[32,1152]{1,0:T(8,128)S(1)} %fusion.33), channel_id=1, source_target_pairs={{496,0},{0,16},{16,32},{32,48},{48,64},{64,80},{80,96},{96,112},{1... | collective-permute-start | bytes 442376 | tf_op jit(solution)/shard_map/while/body/eval_jaxpr/ppermute | solution.py:12
  499.4 12.5 %collective-permute-start.1 = (f32[32,1152]{1,0:T(8,128)S(1)}, f32[32,1152]{1,0:T(8,128)S(1)}, u32[]{:S(2)}, u32[]{:S(2)}) collective-permute-start(f32[32,1152]{1,0:T(8,128)S(1)} %fusion.33), channel_id=1, source_target_pairs={{496,0},{0,16},{16,32},{32,48},{48,64},{64,80},{80,96},{96,112},{1... | collective-permute-start | bytes 442376 | tf_op jit(solution)/shard_map/while/body/eval_jaxpr/ppermute | solution.py:12
  516.7 12.5 %collective-permute-start.1 = (f32[32,1152]{1,0:T(8,128)S(1)}, f32[32,1152]{1,0:T(8,128)S(1)}, u32[]{:S(2)}, u32[]{:S(2)}) collective-permute-start(f32[32,1152]{1,0:T(8,128)S(1)} %fusion.33), channel_id=1, source_target_pairs={{496,0},{0,16},{16,32},{32,48},{48,64},{64,80},{80,96},{96,112},{1... | collective-permute-start | bytes 442376 | tf_op jit(solution)/shard_map/while/body/eval_jaxpr/ppermute | solution.py:12
  585.7 12.5 %collective-permute-start.1 = (f32[32,1152]{1,0:T(8,128)S(1)}, f32[32,1152]{1,0:T(8,128)S(1)}, u32[]{:S(2)}, u32[]{:S(2)}) collective-permute-start(f32[32,1152]{1,0:T(8,128)S(1)} %fusion.33), channel_id=1, source_target_pairs={{496,0},{0,16},{16,32},{32,48},{48,64},{64,80},{80,96},{96,112},{1... | collective-permute-start | bytes 442376 | tf_op jit(solution)/shard_map/while/body/eval_jaxpr/ppermute | solution.py:12
  603.0 12.5 %collective-permute-start.1 = (f32[32,1152]{1,0:T(8,128)S(1)}, f32[32,1152]{1,0:T(8,128)S(1)}, u32[]{:S(2)}, u32[]{:S(2)}) collective-permute-start(f32[32,1152]{1,0:T(8,128)S(1)} %fusion.33), channel_id=1, source_target_pairs={{496,0},{0,16},{16,32},{32,48},{48,64},{64,80},{80,96},{96,112},{1... | collective-permute-start | bytes 442376 | tf_op jit(solution)/shard_map/while/body/eval_jaxpr/ppermute | solution.py:12
  620.2 12.5 %collective-permute-start.1 = (f32[32,1152]{1,0:T(8,128)S(1)}, f32[32,1152]{1,0:T(8,128)S(1)}, u32[]{:S(2)}, u32[]{:S(2)}) collective-permute-start(f32[32,1152]{1,0:T(8,128)S(1)} %fusion.33), channel_id=1, source_target_pairs={{496,0},{0,16},{16,32},{32,48},{48,64},{64,80},{80,96},{96,112},{1... | collective-permute-start | bytes 442376 | tf_op jit(solution)/shard_map/while/body/eval_jaxpr/ppermute | solution.py:12
  (47 other events, 518.1 us)
Sparse Core Ops, SparseCore 0:
  10.1 84.5 all-gather.1
  656.5 90.8 reduce-scatter.3
where the time goes:
time: 767 us; the launch traced here: 754 us
  waiting for transfers between devices  476 us (62%)
  starting transfers between devices  137 us (18%)
  matrix products  69.8 us (9%)
  local copies, waits for them, and re-layouts  52.9 us (7%)
  between operations  14.8 us (2%)
    ppermute x64, waiting for transfers between devices, from_behind(): return lax.ppermute(block, axis, route)  314 us
    ppermute x64, starting transfers between devices, from_behind(): return lax.ppermute(block, axis, route)  127 us
    unnamed x3, waiting for transfers between devices  89.8 us
    all_gather x1, waiting for transfers between devices, body(): text_rows = lax.all_gather(text_feats, 'tensor', axis=1, tiled=True)  67.8 us
    dot_general x32, matrix products, tile_terms(): lax.dot_general(piece, text_hat, (((1,), (1,)), ((), ())), preferred_elem...  55.9 us
    dynamic_slice x32, local copies, waits for them, and re-layouts, groups_of(): lax.dynamic_slice_in_dim(group_ids, anchor * count + tensor_pos * width,...  24.5 us
    dynamic_update_slice x32, local copies, waits for them, and re-layouts, step(): seen = lax.dynamic_update_index_in_dim(seen, piece, turn, 0)  20.4 us
  transfers between devices with their start and end apart: 67, of which 67 were waited for; matrix products, arithmetic and copies ran while one was open for 15% of the time, Pallas kernels for 0%

commit v1 on v0

v1 whole, which is shorter than its diff:
```python
import jax
import jax.numpy as jnp
from jax import lax
from jax.sharding import PartitionSpec as P


def normalize(rows):
    wide = rows.astype(jnp.float32)
    inverse = lax.rsqrt(jnp.sum(wide * wide, axis=1, keepdims=True) + 1e-06)
    return (wide * inverse, inverse)


def unit_back(grad_hat, unit, inverse):
    return (grad_hat - unit * jnp.sum(unit * grad_hat, axis=1, keepdims=True)) * inverse


def body(text_feats, image_feats, group_ids, log_scale, bias):
    scale = jnp.exp(log_scale[0])
    offset = bias[0]
    n_dp = lax.axis_size("dp")
    dp = lax.axis_index("dp")
    tensor = lax.axis_index("tensor")
    feats = jnp.stack([text_feats, image_feats])
    rows = lax.all_to_all(feats, "tensor", split_axis=1, concat_axis=2, tiled=True)
    text_unit, text_inverse = normalize(rows[0])
    image_unit, image_inverse = normalize(rows[1])
    width = rows.shape[1]
    count = text_feats.shape[0]
    text_hat = lax.all_gather(text_unit.astype(jnp.bfloat16), "tensor", axis=0, tiled=True)
    image_hat = lax.all_gather(image_unit.astype(jnp.bfloat16), "dp", axis=0, tiled=True)
    text_groups = lax.dynamic_slice_in_dim(group_ids, dp * count, count, 0)
    image_groups = lax.dynamic_slice_in_dim(
        group_ids.reshape(n_dp, count), tensor * width, width, 1
    ).reshape(-1)
    logits = (
        scale
        * lax.dot_general(
            image_hat, text_hat, (((1,), (1,)), ((), ())), preferred_element_type=jnp.float32
        )
        + offset
    )
    sign = jnp.where(
        image_groups[:, None] == text_groups[None, :], jnp.float32(1.0), jnp.float32(-1.0)
    )
    slope = (-sign * jax.nn.sigmoid(-sign * logits)).astype(jnp.bfloat16)
    image_push = scale * jnp.dot(slope, text_hat, preferred_element_type=jnp.float32)
    text_push = scale * lax.dot_general(
        slope, image_hat, (((0,), (0,)), ((), ())), preferred_element_type=jnp.float32
    )
    image_push = lax.psum_scatter(image_push, "dp", scatter_dimension=0, tiled=True)
    text_push = lax.psum_scatter(text_push, "tensor", scatter_dimension=0, tiled=True)
    image_grad = unit_back(image_push, image_unit, image_inverse)
    text_grad = unit_back(text_push, text_unit, text_inverse)
    text_grad = lax.all_to_all(text_grad, "tensor", split_axis=1, concat_axis=0, tiled=True)
    return (text_grad, image_grad)


def solution(mesh):
    placed = (P("dp", "tensor"), P("dp", "tensor"), P(), P(), P())
    return jax.shard_map(
        body,
        mesh=mesh,
        in_specs=placed,
        out_specs=(P("dp", "tensor"), P(("dp", "tensor"), None)),
        check_vma=False,
    )
```

time: 767 us -> 471 us (0.61); the launches traced: 754 us -> 471 us
  starting transfers between devices: 137 us -> 0.16 us
  waiting for transfers between devices: 476 us -> 397 us
  matrix products: 69.8 us -> 10.9 us
  local copies, waits for them, and re-layouts: 52.9 us -> 3.33 us
  blocking collectives: 0 us -> 36.8 us
    ppermute x64 -> x0, waiting for transfers between devices: 314 us -> none  [from_behind(): return lax.ppermute(block, axis, route)]
    reduce_scatter x0 -> x2, waiting for transfers between devices: none -> 215 us  [the longest x1 143 us: body(): lax.psum_scatter(image_push, 'dp', scatter_dimension=0, tiled=True)]
    ppermute x64 -> x0, starting transfers between devices: 127 us -> none  [from_behind(): return lax.ppermute(block, axis, route)]
    all_gather x1 -> x2, waiting for transfers between devices: 67.8 us -> 182 us  [the longest x1 102 us: body(): lax.all_gather(image_unit.astype(jnp.bfloat16), 'dp', axis=0, tiled=True)]
    unnamed x3 -> x4, waiting for transfers between devices: 89.8 us -> 0.07 us
    dot_general x65 -> x3, matrix products: 69.8 us -> 10.9 us  [the longest x1 4.25 us: body(): lax.dot_general(image_hat, text_hat, (((1,), (1,)), ((), ())), preferred_...]
    all_to_all x0 -> x2, blocking collectives: none -> 36.8 us  [the longest x1 18.6 us: body(): lax.all_to_all(text_grad, 'tensor', split_axis=1, concat_axis=0, tiled=True)]
    dynamic_slice x33 -> x2, local copies, waits for them, and re-layouts: 25.2 us -> 0.15 us  [the longest x1 0.08 us: body(): text_groups = lax.dynamic_slice_in_dim(group_ids, dp * count, count, 0)]
  transfers between devices with their start and end apart: 67 -> 4, of which waited for: 67 -> 4; matrix products, arithmetic and copies ran while one was open for 15% -> 2% of each run, Pallas kernels for 0% -> 0%
where the time goes in v1:
time: 471 us
  waiting for transfers between devices  397 us (84%)
  blocking collectives  36.8 us (8%)
  between operations  15.2 us (3%)
  matrix products  10.9 us (2%)
  other arithmetic  7.48 us (2%)
    reduce_scatter x1, waiting for transfers between devices, body(): lax.psum_scatter(image_push, 'dp', scatter_dimension=0, tiled=True)  143 us
    all_gather x1, waiting for transfers between devices, body(): lax.all_gather(image_unit.astype(jnp.bfloat16), 'dp', axis=0, tiled=True)  102 us
    all_gather x1, waiting for transfers between devices, body(): lax.all_gather(text_unit.astype(jnp.bfloat16), 'tensor', axis=0, tiled=True)  79.6 us
    reduce_scatter x1, waiting for transfers between devices, body(): lax.psum_scatter(text_push, 'tensor', scatter_dimension=0, tiled=True)  71.5 us
    all_to_all x1, blocking collectives, body(): lax.all_to_all(text_grad, 'tensor', split_axis=1, concat_axis=0, tiled=True)  18.6 us
    all_to_all x1, blocking collectives, body(): lax.all_to_all(feats, 'tensor', split_axis=1, concat_axis=2, tiled=True)  18.3 us
  transfers between devices with their start and end apart: 4, of which 4 were waited for; matrix products, arithmetic and copies ran while one was open for 2% of the time, Pallas kernels for 0%

profile of v1, /device:TPU:6, one launch (start us, length us, event | category | flops | bytes accessed | tf_op | source)
XLA Modules:
  0.0 470.9 jit_solution(9812612473015506161)
XLA Ops:
  7.2 0.9 pad_maximum_fusion
  8.1 0.2 copy.22
  8.3 18.3 %all_to_all.34 = bf16[2,512,72]{2,0,1:T(2,128)(2,1)S(1)} all-to-all(bf16[2,512,72]{2,0,1:T(2,128)(2,1)S(1)} %copy.22), channel_id=1, replica_groups=mesh['dp'=32,'tensor'=16] {'tensor'}, dimensions={1} | all-to-all | bytes 294912 | tf_op jit(solution)/shard_map/all_to_all | solution.py:24
  26.6 0.2 multiply_reduce_fusion
  26.9 0.2 copy.25
  27.0 0.1 reshape.37
  27.2 0.7 multiply_convert_fusion.1
  28.0 0.2 copy.24
  28.3 0.7 multiply_convert_fusion.2
  30.7 79.6 %all-gather.5.cloned.1.call-done = bf16[512,1152]{1,0:T(8,128)(2,1)} async-done(((bf16[32,1152]{1,0:T(8,128)(2,1)}), bf16[512,1152]{1,0:T(8,128)(2,1)}) %all-gather.5.cloned.1.call-update) | async-done | bytes 1179664 | tf_op jit(solution)/shard_map/all_gather | solution.py:29
  110.3 102.4 %all-gather.3.cloned.1.call-done = bf16[1024,1152]{1,0:T(8,128)(2,1)} async-done(((bf16[32,1152]{1,0:T(8,128)(2,1)}), bf16[1024,1152]{1,0:T(8,128)(2,1)}) %all-gather.3.cloned.1.call-update) | async-done | bytes 2359312 | tf_op jit(solution)/shard_map/all_gather | solution.py:30
  212.7 4.3 multiply_convert_fusion
  216.9 3.0 convolution_multiply_fusion.1
  220.0 1.2 copy-done.1
  221.2 3.6 convolution_multiply_fusion
  224.9 71.5 %reduce-scatter.3.cloned.1.call-done = f32[32,1152]{1,0:T(8,128)} async-done(((f32[512,1152]{1,0:T(8,128)}), f32[32,1152]{1,0:T(8,128)}) %reduce-scatter.3.cloned.1.call-update) | async-done | bytes 147472 | tf_op jit(solution)/shard_map/reduce_scatter | solution.py:51
  296.4 1.1 multiply_reduce_fusion.3
  297.5 1.0 subtract_multiply_fusion.1
  298.5 0.2 all_to_all.28
  298.8 18.6 %all_to_all.35 = f32[32,16,72]{2,0,1:T(8,128)S(1)} all-to-all(f32[32,16,72]{2,0,1:T(8,128)S(1)} %copy.26), channel_id=1, replica_groups=mesh['dp'=32,'tensor'=16] {'tensor'}, dimensions={1} | all-to-all | bytes 294912 | tf_op jit(solution)/shard_map/all_to_all | solution.py:54
  317.4 0.8 copy.27
  318.1 143.5 %reduce-scatter.5.cloned.1.call-done = f32[32,1152]{1,0:T(8,128)} async-done(((f32[1024,1152]{1,0:T(8,128)}), f32[32,1152]{1,0:T(8,128)}) %reduce-scatter.5.cloned.1.call-update) | async-done | bytes 147472 | tf_op jit(solution)/shard_map/reduce_scatter | solution.py:50
  461.6 1.1 multiply_reduce_fusion.2
  462.7 1.7 subtract_multiply_fusion
  (23 shorter events, 0.8 us)
Async XLA Ops:
  7.2 103.1 %all-gather.5.cloned.1.call-start = ((), (), s32[]{:S(2)}) async-start(), calls=%async_computation.5 | async-start | bytes 1253376 | tf_op jit(solution)/shard_map/all_gather | solution.py:29
  26.6 3.8 copy-start.2
  27.9 184.7 %all-gather.3.cloned.1.call-start = ((), (), s32[]{:S(2)}) async-start(), calls=%async_computation.4 | async-start | bytes 2433024 | tf_op jit(solution)/shard_map/all_gather | solution.py:30
  29.0 267.3 %reduce-scatter.3.cloned.1.call-start = ((), (), s32[]{:S(2)}) async-start(), calls=%async_computation.6 | async-start | bytes 2506752 | tf_op jit(solution)/shard_map/reduce_scatter | solution.py:51
  212.7 4.3 copy-start
  220.0 1.3 copy-start.1
  220.0 241.6 %reduce-scatter.5.cloned.1.call-start = ((), (), s32[]{:S(2)}) async-start(), calls=%async_computation.7 | async-start | bytes 4866048 | tf_op jit(solution)/shard_map/reduce_scatter | solution.py:50
Sparse Core Ops, SparseCore 0:
  28.0 82.1 all-gather.4
  114.1 98.4 all-gather.2
  220.1 76.2 reduce-scatter.2
  301.1 160.5 reduce-scatter.4

commit v2 on v1

v2 whole, which is shorter than its diff:
```python
import jax
import jax.numpy as jnp
from jax import lax
from jax.experimental import pallas as pl
from jax.experimental.pallas import tpu as pltpu
from jax.sharding import PartitionSpec as P

MESH = pl.DeviceIdType.MESH
F32 = jnp.float32
BF16 = jnp.bfloat16

D = 1152
W = 32
NT = 16
C = D // NT
COPIES = 160

PLACE = {0: 0, 1: 1, 7: 2, 2: 3, 6: 4, 3: 5, 5: 6, 4: 7}


def device_at(y, z, core, x):
    return (y * 4 + (z // 4) * 2 + core, (z % 4) * 4 + x)


def kernel(
    text_ref, image_ref, ids_ref, log_scale_ref, bias_ref,
    text_out, image_out,
    text_slabs, image_slabs, rows32, text_unit, image_unit,
    txt, img, text_ids, image_ids, slopes,
    text_sum, chain_out, chain_in, pair_out, pair_in,
    image_sum, core_out, core_in, x_out, x_in, z_out, z_in, slices,
    send_sem, recv_sem, local_sem,
):
    dp, tensor = lax.axis_index("dp"), lax.axis_index("tensor")
    y, core = dp // 4, dp % 2
    z = ((dp // 2) % 2) * 4 + tensor // 4
    x = tensor % 4
    parity = z % 2

    def along(dy=0, dz=0, dx=0, flip=False):
        return device_at((y + dy) % 8, (z + dz) % 8, (1 - core) if flip else core, (x + dx) % 4)

    z_mate = device_at(y, z + 1 - 2 * parity, core, x)
    core_mate = along(flip=True)

    def mate(k):
        return (dp, (tensor + k) % NT)

    copies = []

    def remote(src, dst, device):
        index = len(copies)
        copy = pltpu.make_async_remote_copy(
            src_ref=src, dst_ref=dst, send_sem=send_sem.at[index], recv_sem=recv_sem.at[index],
            device_id=device, device_id_type=MESH,
        )
        copies.append(copy)
        copy.start()
        return copy

    barrier = pltpu.get_barrier_semaphore()
    greeted = [mate(k) for k in range(1, NT)]
    greeted += [core_mate, along(dy=1), along(dy=7), along(dz=4)]
    outside = device_at(y, (z + 2 + 4 * (1 - (z % 4) // 2)) % 8, core, x)
    greeted += [outside]
    for device in greeted:
        pl.semaphore_signal(barrier, inc=1, device_id=device, device_id_type=MESH)

    own_rows = pl.ds(pl.multiple_of(tensor * W, W), W)
    own_text = pltpu.make_async_copy(text_ref.at[own_rows], text_slabs.at[tensor], local_sem.at[0])
    own_image = pltpu.make_async_copy(image_ref.at[own_rows], image_slabs.at[tensor], local_sem.at[1])
    own_text.start()
    own_image.start()

    def id_row(y_at, z_at, core_at):
        at = (y_at * 4 + (z_at // 4) * 2 + core_at) * 4 + z_at % 4
        return ids_ref[pl.ds(at, 1), :]

    lane = lax.broadcasted_iota(jnp.int32, (W, 128), 1)
    row = lax.broadcasted_iota(jnp.int32, (W, 128), 0)
    own_lane = lane == row + x * W
    for r, place in PLACE.items():
        for p in range(2):
            z_at = z if p == 0 else z + 1 - 2 * parity
            ids = jnp.broadcast_to(id_row((y + r) % 8, z_at, core), (W, 128))
            at = (place * 2 + p) * W
            text_ids[at : at + W, :] = jnp.sum(
                jnp.where(own_lane, ids, 0), axis=1, keepdims=True
            )
    for c in range(2):
        for q in range(4):
            ids = id_row(y, (z + 2 * q) % 8, core if c == 0 else 1 - core)
            turned = ids
            for k in range(1, 4):
                rolled = jnp.concatenate([ids[:, k * W :], ids[:, : k * W]], axis=1)
                turned = jnp.where(x == k, rolled, turned)
            at = (c * 4 + q) * 128
            image_ids[:, at : at + 128] = turned

    scale = jnp.exp(jnp.full((1, 128), log_scale_ref[0], F32))[:, :1]
    offset = bias_ref[0]

    pl.semaphore_wait(barrier, len(greeted))

    def exchange(feats, slabs):
        out = []
        for k in range(1, NT):
            there = (tensor + k) % NT
            out.append(
                remote(
                    feats.at[pl.ds(pl.multiple_of(there * W, W), W)], slabs.at[tensor], mate(k)
                )
            )
        return out

    def normalize(slabs, unit_ref):
        total = jnp.zeros((W, 1), F32)
        for j in range(NT):
            wide = slabs[j].astype(F32)
            rows32[:, j * C : (j + 1) * C] = wide
            total = total + jnp.sum(wide * wide, axis=1, keepdims=True)
        inverse = lax.rsqrt(total + 1e-06)
        unit = rows32[...] * inverse
        unit_ref[...] = unit
        return unit.astype(BF16), inverse

    text_pieces = exchange(text_ref, text_slabs)
    image_pieces = exchange(image_ref, image_slabs)

    own_text.wait()
    for copy in text_pieces:
        copy.wait_recv()
    hat, text_inverse = normalize(text_slabs, text_unit)
    txt[0, 0] = hat

    def text_slot(r, p):
        return txt.at[PLACE[r], p]

    def forward(r, p):
        arrive = {}
        if r == 0 or (r > 4 and (r > 5 or p == 0)):
            arrive[(r - 1) % 8] = remote(text_slot(r, p), text_slot((r - 1) % 8, p), along(dy=1))
        if r == 0 or (r < 4 and (r < 3 or p == 1)):
            arrive[r + 1] = remote(text_slot(r, p), text_slot(r + 1, p), along(dy=7))
        return arrive

    pair = remote(text_slot(0, 0), text_slot(0, 1), z_mate)
    waiting = {(r, 0): copy for r, copy in forward(0, 0).items()}

    def text_step(r, p):
        waiting.pop((r, p)).wait_recv()
        waiting.update({(s, p): copy for s, copy in forward(r, p).items()})

    own_image.wait()
    for copy in image_pieces:
        copy.wait_recv()
    hat, image_inverse = normalize(image_slabs, image_unit)
    img[0, 0, 0] = hat
    z_wait = {}
    x_wait = {}
    for q in (1, 3, 2):
        z_wait[q] = remote(img.at[0, 0, 0], img.at[0, q, 0], along(dz=-2 * q))

    def spread_x(q):
        for k in (1, 3, 2):
            x_wait[(q, k)] = remote(img.at[0, q, 0], img.at[0, q, k], along(dx=-k))

    core_wait = {}

    def to_core(q):
        for k in (1, 3, 2):
            x_wait.pop((q, k)).wait_recv()
        core_wait[q] = remote(img.at[0, q], img.at[1, q], core_mate)

    spread_x(0)
    pair.wait_recv()
    waiting.update({(s, 1): copy for s, copy in forward(0, 1).items()})
    text_step(7, 0)
    text_step(1, 0)
    for q in (1, 3):
        z_wait[q].wait_recv()
        spread_x(q)
    text_step(7, 1)
    text_step(1, 1)
    z_wait[2].wait_recv()
    spread_x(2)
    text_step(6, 0)
    text_step(2, 0)
    to_core(0)
    text_step(6, 1)
    text_step(2, 1)
    to_core(1)
    text_step(5, 0)
    text_step(3, 1)
    to_core(3)
    text_step(5, 1)
    text_step(3, 0)
    to_core(2)

    def tile(batch, c, half):
        rows = txt[4 * batch : 4 * batch + 4].reshape(256, D)
        cols = img[c, 2 * half : 2 * half + 2].reshape(256, D)
        at = c * 512 + half * 256
        logits = (
            scale
            * lax.dot_general(rows, cols, (((1,), (1,)), ((), ())), preferred_element_type=F32)
            + offset
        )
        same = text_ids[batch * 256 : batch * 256 + 256, :] == image_ids[:, at : at + 256]
        share = 1.0 / (1.0 + jnp.exp(jnp.where(same, logits, -logits)))
        slopes[batch * 256 : batch * 256 + 256, at : at + 256] = jnp.where(
            same, -share, share
        ).astype(BF16)

    def text_push(batch):
        push = jnp.dot(
            slopes[batch * 256 : batch * 256 + 256, :], img[...].reshape(1024, D),
            preferred_element_type=F32,
        )
        text_sum[4 * batch : 4 * batch + 4] = push.reshape(4, 2, W, D)

    for q in range(4):
        core_wait[q].wait_recv()
    for c in range(2):
        for half in range(2):
            tile(0, c, half)
    text_push(0)
    text_step(4, 0)
    text_step(4, 1)
    for c in range(2):
        for half in range(2):
            tile(1, c, half)
    text_push(1)

    chains = (
        (0, 0, (4, 3, 2, 1)),
        (1, 1, (4, 5, 6, 7)),
        (0, 1, (3, 2, 1)),
        (1, 0, (5, 6, 7)),
    )
    arrived = {}

    def chain_step(number, hop):
        way, p, slots = chains[number]
        part = text_sum[PLACE[slots[hop]], p]
        if hop:
            arrived[number].wait_recv()
            part = part + chain_in[number, hop - 1].astype(F32)
        chain_out[number, hop] = part.astype(BF16)
        arrived[number] = remote(
            chain_out.at[number, hop], chain_in.at[number, hop], along(dy=1 if way == 0 else 7)
        )

    for number in range(4):
        chain_step(number, 0)

    def image_push(c, half):
        at = c * 512 + half * 256
        return lax.dot_general(
            slopes[:, at : at + 256], txt[...].reshape(512, D),
            (((0,), (0,)), ((), ())), preferred_element_type=F32,
        ).reshape(2, 4, W, D)

    core_sums = []
    for half in (1, 0):
        core_out[2 * half : 2 * half + 2] = image_push(1, half).astype(BF16)
        core_sums.append(
            remote(core_out.at[pl.ds(2 * half, 2)], core_in.at[pl.ds(2 * half, 2)], core_mate)
        )
    for number in range(4):
        chain_step(number, 1)
    x_sums = {}
    z_sums = {}

    def x_send(q):
        for k in (2, 1, 3):
            x_out[q, k] = (image_sum[q, k] + core_in[q, k].astype(F32)).astype(BF16)
            x_sums[(q, k)] = remote(x_out.at[q, k], x_in.at[q, k], along(dx=k))

    def z_part(q):
        part = image_sum[q, 0] + core_in[q, 0].astype(F32)
        for k in (2, 1, 3):
            x_sums[(q, k)].wait_recv()
            part = part + x_in[q, k].astype(F32)
        return part

    def z_send(q):
        z_out[q] = z_part(q).astype(BF16)
        z_sums[q] = remote(z_out.at[q], z_in.at[q], along(dz=2 * q))

    for number, half in enumerate((1, 0)):
        image_sum[2 * half : 2 * half + 2] = image_push(0, half)
        core_sums[number].wait_recv()
        x_send(2 * half + 0)
        x_send(2 * half + 1)
    for number in range(4):
        chain_step(number, 2)
    z_send(2)
    z_send(3)
    for number in range(2):
        chain_step(number, 3)
    z_send(1)

    def gathered(p):
        total = text_sum[0, p]
        for number, (way, chain_p, slots) in enumerate(chains):
            if chain_p == p:
                arrived[number].wait_recv()
                total = total + chain_in[number, len(slots) - 1].astype(F32)
        return total

    def unit_back(push, unit, inverse):
        push = push * scale
        return (push - unit * jnp.sum(unit * push, axis=1, keepdims=True)) * inverse

    pair_out[...] = gathered(1).astype(BF16)
    mate_sum = remote(pair_out, pair_in, z_mate)
    push = gathered(0)
    mate_sum.wait_recv()
    grad = unit_back(push + pair_in[...].astype(F32), text_unit[...], text_inverse)
    for j in range(NT):
        slices[j] = grad[:, j * C : (j + 1) * C]
    back = []
    for k in range(1, NT):
        back.append(
            remote(slices.at[(tensor + k) % NT], text_out.at[own_rows], mate(k))
        )
    text_out[own_rows, :] = slices[tensor]

    push = z_part(0)
    for q in (1, 3, 2):
        z_sums[q].wait_recv()
        push = push + z_in[q].astype(F32)
    image_out[...] = unit_back(push, image_unit[...], image_inverse)

    for copy in back:
        copy.wait_recv()
    for copy in copies:
        copy.wait_send()


def body(text_feats, image_feats, group_ids, log_scale, bias):
    anywhere = pl.BlockSpec(memory_space=pl.ANY)
    vmem = pl.BlockSpec(memory_space=pltpu.VMEM)
    smem = pl.BlockSpec(memory_space=pltpu.SMEM)
    block = (W, D)
    return pl.pallas_call(
        kernel,
        out_shape=(
            jax.ShapeDtypeStruct((NT * W, C), F32),
            jax.ShapeDtypeStruct(block, F32),
        ),
        in_specs=[anywhere, anywhere, vmem, smem, smem],
        out_specs=(vmem, vmem),
        scratch_shapes=[
            pltpu.VMEM((NT, W, C), BF16),
            pltpu.VMEM((NT, W, C), BF16),
            pltpu.VMEM(block, F32),
            pltpu.VMEM(block, F32),
            pltpu.VMEM(block, F32),
            pltpu.VMEM((8, 2) + block, BF16),
            pltpu.VMEM((2, 4, 4) + block, BF16),
            pltpu.VMEM((512, 1), jnp.int32),
            pltpu.VMEM((1, 1024), jnp.int32),
            pltpu.VMEM((512, 1024), BF16),
            pltpu.VMEM((8, 2) + block, F32),
            pltpu.VMEM((4, 4) + block, BF16),
            pltpu.VMEM((4, 4) + block, BF16),
            pltpu.VMEM(block, BF16),
            pltpu.VMEM(block, BF16),
            pltpu.VMEM((4, 4) + block, F32),
            pltpu.VMEM((4, 4) + block, BF16),
            pltpu.VMEM((4, 4) + block, BF16),
            pltpu.VMEM((4, 4) + block, BF16),
            pltpu.VMEM((4, 4) + block, BF16),
            pltpu.VMEM((4,) + block, BF16),
            pltpu.VMEM((4,) + block, BF16),
            pltpu.VMEM((NT, W, C), F32),
            pltpu.SemaphoreType.DMA((COPIES,)),
            pltpu.SemaphoreType.DMA((COPIES,)),
            pltpu.SemaphoreType.DMA((2,)),
        ],
        compiler_params=pltpu.CompilerParams(
            collective_id=0, has_side_effects=True, vmem_limit_bytes=50 * 2**20
        ),
    )(text_feats, image_feats, group_ids.reshape(128, 128), log_scale, bias)


def solution(mesh):
    placed = (P("dp", "tensor"), P("dp", "tensor"), P(), P(), P())
    return jax.shard_map(
        body,
        mesh=mesh,
        in_specs=placed,
        out_specs=(P("dp", "tensor"), P(("dp", "tensor"), None)),
        check_vma=False,
    )
```

time: 471 us -> 85.4 us (0.18)
  waiting for transfers between devices: 397 us -> 0 us
  Pallas kernels: 0 us -> 79.9 us
  blocking collectives: 36.8 us -> 0 us
  between operations: 15.2 us -> 1.97 us
  matrix products: 10.9 us -> 0 us
  other arithmetic: 7.48 us -> 0 us
    reduce_scatter x2 -> x0, waiting for transfers between devices: 215 us -> none  [the longest x1 143 us: body(): lax.psum_scatter(image_push, 'dp', scatter_dimension=0, tiled=True)]
    all_gather x2 -> x0, waiting for transfers between devices: 182 us -> none  [the longest x1 102 us: body(): lax.all_gather(image_unit.astype(jnp.bfloat16), 'dp', axis=0, tiled=True)]
    pallas_call x0 -> x1, Pallas kernels: none -> 79.9 us  [body(): pl.pallas_call(kernel, out_shape=(jax.ShapeDtypeStruct((NT * W, C), F32),...]
    all_to_all x2 -> x0, blocking collectives: 36.8 us -> none  [the longest x1 18.6 us: body(): lax.all_to_all(text_grad, 'tensor', split_axis=1, concat_axis=0, tiled=True)]
    dot_general x3 -> x0, matrix products: 10.9 us -> none  [the longest x1 4.25 us: body(): lax.dot_general(image_hat, text_hat, (((1,), (1,)), ((), ())), preferred_...]
  transfers between devices with their start and end apart: 4 -> 0, of which waited for: 4 -> 0; matrix products, arithmetic and copies ran while one was open for 2% -> 0% of each run, Pallas kernels for 0% -> 0%
where the time goes in v2:
time: 85.4 us; the launch traced here: 85.2 us
  Pallas kernels  79.9 us (94%)
  local copies, waits for them, and re-layouts  3.31 us (4%)
  between operations  1.97 us (2%)
    pallas_call x1, Pallas kernels, body(): pl.pallas_call(kernel, out_shape=(jax.ShapeDtypeStruct((NT * W, C), F32),...  79.9 us
    unnamed x7, local copies, waits for them, and re-layouts  2.53 us

profile of v2, /device:TPU:6, one launch (start us, length us, event | category | flops | bytes accessed | tf_op | source)
XLA Modules:
  0.0 85.2 jit_solution(12877028132737744285)
XLA Ops:
  1.9 0.0 copy-start.1
  1.9 1.0 %copy.7.text_ref = bf16[512,72]{1,0:T(8,128)(2,1)S(1)} copy(bf16[512,72]{0,1:T(8,128)(2,1)} %param.5) | data formatting | bytes 147456 | tf_op args[0]
  3.0 0.0 copy-done.1
  3.0 0.0 copy-start
  3.0 0.1 copy.8.image_ref
  3.1 0.7 copy-done
  3.8 79.9 %shard_map.68 = (f32[512,72]{1,0:T(8,128)S(1)}, f32[32,1152]{1,0:T(8,128)S(1)}) custom-call(bf16[512,72]{1,0:T(8,128)(2,1)S(1)} %copy.7.text_ref, bf16[512,72]{1,0:T(8,128)(2,1)S(1)} %copy.8.image_ref, s32[128,128]{1,0:T(8,128)S(1)} %bitcast.1, f32[1]{0:T(128)S(6)} %copy.11.log_scale_ref, f32[1]{0:T(128)S(6)} %copy.12.bias_ref), custom_call_target="tpu_custom_call" | custom-call | tf_op jit(solution)/shard_map/pallas_call | solution.py:347
  83.8 0.8 copy.9
  84.5 0.7 copy.13
Async XLA Ops:
  1.9 1.1 %copy-start.1 = (bf16[512,72]{0,1:T(8,128)(2,1)S(1)}, bf16[512,72]{0,1:T(8,128)(2,1)}, u32[]{:S(2)}) copy-start(bf16[512,72]{0,1:T(8,128)(2,1)} %param.6) | copy-start | bytes 221188
  3.0 0.8 copy-start

commit v3 on v2

--- a/solution.py
+++ b/solution.py
@@ -23,12 +23,14 @@
 
 
 def kernel(
-    text_ref, image_ref, ids_ref, log_scale_ref, bias_ref,
+    text_hbm, image_hbm, ids_hbm, log_scale_ref, bias_ref,
     text_out, image_out,
-    text_slabs, image_slabs, rows32, text_unit, image_unit,
+    text_own, image_own, ids, cols_out, cols_in, turned, rows_out, rows_in,
+    rows32, text_unit, image_unit,
     txt, img, text_ids, image_ids, slopes,
     text_sum, chain_out, chain_in, pair_out, pair_in,
-    image_sum, core_out, core_in, x_out, x_in, z_out, z_in, slices,
+    image_sum, core_out, core_in, x_out, x_in, z_out, z_in,
+    grad_out, grad_in, back_out,
     send_sem, recv_sem, local_sem,
 ):
     dp, tensor = lax.axis_index("dp"), lax.axis_index("tensor")
@@ -40,11 +42,12 @@
     def along(dy=0, dz=0, dx=0, flip=False):
         return device_at((y + dy) % 8, (z + dz) % 8, (1 - core) if flip else core, (x + dx) % 4)
 
+    z_lo = z % 4
     z_mate = device_at(y, z + 1 - 2 * parity, core, x)
     core_mate = along(flip=True)
 
-    def mate(k):
-        return (dp, (tensor + k) % NT)
+    def z_run(k):
+        return device_at(y, z - z_lo + (z_lo + k) % 4, core, x)
 
     copies = []
 
@@ -58,23 +61,37 @@
         copy.start()
         return copy
 
+    loads = [
+        pltpu.make_async_copy(src, dst, local_sem.at[n])
+        for n, (src, dst) in enumerate(
+            ((text_hbm, text_own), (image_hbm, image_own), (ids_hbm, ids))
+        )
+    ]
+    for load in loads:
+        load.start()
+
     barrier = pltpu.get_barrier_semaphore()
-    greeted = [mate(k) for k in range(1, NT)]
+    greeted = [z_run(k) for k in (1, 2, 3)] + [along(dx=k) for k in (1, 2, 3)]
     greeted += [core_mate, along(dy=1), along(dy=7), along(dz=4)]
-    outside = device_at(y, (z + 2 + 4 * (1 - (z % 4) // 2)) % 8, core, x)
-    greeted += [outside]
+    greeted += [device_at(y, (z + 2 + 4 * (1 - z_lo // 2)) % 8, core, x)]
     for device in greeted:
         pl.semaphore_signal(barrier, inc=1, device_id=device, device_id_type=MESH)
 
-    own_rows = pl.ds(pl.multiple_of(tensor * W, W), W)
-    own_text = pltpu.make_async_copy(text_ref.at[own_rows], text_slabs.at[tensor], local_sem.at[0])
-    own_image = pltpu.make_async_copy(image_ref.at[own_rows], image_slabs.at[tensor], local_sem.at[1])
-    own_text.start()
-    own_image.start()
+    for load in loads:
+        load.wait()
+    for kind, own in enumerate((text_own, image_own)):
+        for run in range(4):
+            piece = own[:, run * 128 : run * 128 + 128].astype(F32)
+            cols_out[run, kind] = jnp.concatenate([piece, jnp.zeros((8, 128), F32)], axis=0).astype(BF16)
+    pl.semaphore_wait(barrier, len(greeted))
+    run_pieces = [
+        remote(cols_out.at[(z_lo + k) % 4], cols_in.at[z_lo], z_run(k)) for k in (1, 3, 2)
+    ]
+    cols_in[z_lo] = cols_out[z_lo]
 
     def id_row(y_at, z_at, core_at):
         at = (y_at * 4 + (z_at // 4) * 2 + core_at) * 4 + z_at % 4
-        return ids_ref[pl.ds(at, 1), :]
+        return ids[pl.ds(at, 1), :]
 
     lane = lax.broadcasted_iota(jnp.int32, (W, 128), 1)
     row = lax.broadcasted_iota(jnp.int32, (W, 128), 0)
@@ -82,55 +99,50 @@
     for r, place in PLACE.items():
         for p in range(2):
             z_at = z if p == 0 else z + 1 - 2 * parity
-            ids = jnp.broadcast_to(id_row((y + r) % 8, z_at, core), (W, 128))
+            here = jnp.broadcast_to(id_row((y + r) % 8, z_at, core), (W, 128))
             at = (place * 2 + p) * W
             text_ids[at : at + W, :] = jnp.sum(
-                jnp.where(own_lane, ids, 0), axis=1, keepdims=True
+                jnp.where(own_lane, here, 0), axis=1, keepdims=True
             )
     for c in range(2):
         for q in range(4):
-            ids = id_row(y, (z + 2 * q) % 8, core if c == 0 else 1 - core)
-            turned = ids
+            here = id_row(y, (z + 2 * q) % 8, core if c == 0 else 1 - core)
+            from_x = here
             for k in range(1, 4):
-                rolled = jnp.concatenate([ids[:, k * W :], ids[:, : k * W]], axis=1)
-                turned = jnp.where(x == k, rolled, turned)
+                rolled = jnp.concatenate([here[:, k * W :], here[:, : k * W]], axis=1)
+                from_x = jnp.where(x == k, rolled, from_x)
             at = (c * 4 + q) * 128
-            image_ids[:, at : at + 128] = turned
+            image_ids[:, at : at + 128] = from_x
 
     scale = jnp.exp(jnp.full((1, 128), log_scale_ref[0], F32))[:, :1]
     offset = bias_ref[0]
 
-    pl.semaphore_wait(barrier, len(greeted))
-
-    def exchange(feats, slabs):
-        out = []
-        for k in range(1, NT):
-            there = (tensor + k) % NT
-            out.append(
-                remote(
-                    feats.at[pl.ds(pl.multiple_of(there * W, W), W)], slabs.at[tensor], mate(k)
-                )
-            )
-        return out
-
-    def normalize(slabs, unit_ref):
+    for copy in run_pieces:
+        copy.wait_recv()
+    for kind in range(2):
+        for run in range(4):
+            turned[run * C : run * C + C, :] = cols_in[run, kind].astype(F32)[:C]
+        turned[4 * C :, :] = jnp.zeros((384 - 4 * C, 128), F32)
+        rows_out[:, kind] = turned[...].T.astype(BF16).reshape(4, W, 384)
+    x_pieces = [
+        remote(rows_out.at[(x + k) % 4], rows_in.at[x], along(dx=k)) for k in (1, 3, 2)
+    ]
+    rows_in[x] = rows_out[x]
+    for copy in x_pieces:
+        copy.wait_recv()
+
+    def normalize(kind, unit_ref):
         total = jnp.zeros((W, 1), F32)
-        for j in range(NT):
-            wide = slabs[j].astype(F32)
-            rows32[:, j * C : (j + 1) * C] = wide
+        for j in range(4):
+            wide = rows_in[j, kind].astype(F32)[:, : 4 * C]
+            rows32[:, j * 4 * C : (j + 1) * 4 * C] = wide
             total = total + jnp.sum(wide * wide, axis=1, keepdims=True)
         inverse = lax.rsqrt(total + 1e-06)
         unit = rows32[...] * inverse
         unit_ref[...] = unit
         return unit.astype(BF16), inverse
 
-    text_pieces = exchange(text_ref, text_slabs)
-    image_pieces = exchange(image_ref, image_slabs)
-
-    own_text.wait()
-    for copy in text_pieces:
-        copy.wait_recv()
-    hat, text_inverse = normalize(text_slabs, text_unit)
+    hat, text_inverse = normalize(0, text_unit)
     txt[0, 0] = hat
 
     def text_slot(r, p):
@@ -151,10 +163,7 @@
         waiting.pop((r, p)).wait_recv()
         waiting.update({(s, p): copy for s, copy in forward(r, p).items()})
 
-    own_image.wait()
-    for copy in image_pieces:
-        copy.wait_recv()
-    hat, image_inverse = normalize(image_slabs, image_unit)
+    hat, image_inverse = normalize(1, image_unit)
     img[0, 0, 0] = hat
     z_wait = {}
     x_wait = {}
@@ -261,14 +270,6 @@
             (((0,), (0,)), ((), ())), preferred_element_type=F32,
         ).reshape(2, 4, W, D)
 
-    core_sums = []
-    for half in (1, 0):
-        core_out[2 * half : 2 * half + 2] = image_push(1, half).astype(BF16)
-        core_sums.append(
-            remote(core_out.at[pl.ds(2 * half, 2)], core_in.at[pl.ds(2 * half, 2)], core_mate)
-        )
-    for number in range(4):
-        chain_step(number, 1)
     x_sums = {}
     z_sums = {}
 
@@ -288,18 +289,28 @@
         z_out[q] = z_part(q).astype(BF16)
         z_sums[q] = remote(z_out.at[q], z_in.at[q], along(dz=2 * q))
 
-    for number, half in enumerate((1, 0)):
+    core_sums = []
+    for half in (1, 0):
+        core_out[2 * half : 2 * half + 2] = image_push(1, half).astype(BF16)
+        core_sums.append(
+            remote(core_out.at[pl.ds(2 * half, 2)], core_in.at[pl.ds(2 * half, 2)], core_mate)
+        )
+    for half in (1, 0):
         image_sum[2 * half : 2 * half + 2] = image_push(0, half)
-        core_sums[number].wait_recv()
-        x_send(2 * half + 0)
-        x_send(2 * half + 1)
+    for number in range(4):
+        chain_step(number, 1)
+    core_sums[0].wait_recv()
+    x_send(2)
+    x_send(3)
+    core_sums[1].wait_recv()
+    x_send(1)
+    x_send(0)
     for number in range(4):
         chain_step(number, 2)
+    for number in range(2):
+        chain_step(number, 3)
     z_send(2)
     z_send(3)
-    for number in range(2):
-        chain_step(number, 3)
-    z_send(1)
 
     def gathered(p):
         total = text_sum[0, p]
@@ -315,25 +326,39 @@
 
     pair_out[...] = gathered(1).astype(BF16)
     mate_sum = remote(pair_out, pair_in, z_mate)
+    z_send(1)
     push = gathered(0)
     mate_sum.wait_recv()
     grad = unit_back(push + pair_in[...].astype(F32), text_unit[...], text_inverse)
-    for j in range(NT):
-        slices[j] = grad[:, j * C : (j + 1) * C]
-    back = []
-    for k in range(1, NT):
-        back.append(
-            remote(slices.at[(tensor + k) % NT], text_out.at[own_rows], mate(k))
-        )
-    text_out[own_rows, :] = slices[tensor]
-
-    push = z_part(0)
+    blank = jnp.zeros((W, 384 - 4 * C), F32)
+    for j in range(4):
+        grad_out[j] = jnp.concatenate([grad[:, j * 4 * C : (j + 1) * 4 * C], blank], axis=1)
+    x_back = [
+        remote(grad_out.at[(x + k) % 4], grad_in.at[x], along(dx=k)) for k in (1, 3, 2)
+    ]
+    grad_in[x] = grad_out[x]
+    image_push_total = z_part(0)
+    for copy in x_back:
+        copy.wait_recv()
+    down = grad_in[...].reshape(128, 384).T
+    for run in range(4):
+        back_out[run] = down[run * C : run * C + C]
+    lanes = pl.ds(pl.multiple_of(z_lo * 128, 128), 128)
+    z_back = [
+        remote(back_out.at[(z_lo + k) % 4], text_out.at[:, lanes], z_run(k)) for k in (1, 3, 2)
+    ]
+    text_out[:, lanes] = back_out[z_lo]
+
     for q in (1, 3, 2):
         z_sums[q].wait_recv()
-        push = push + z_in[q].astype(F32)
-    image_out[...] = unit_back(push, image_unit[...], image_inverse)
-
-    for copy in back:
+        image_push_total = image_push_total + z_in[q].astype(F32)
+    grad = unit_back(image_push_total, image_unit[...], image_inverse)
+    for j in range(4):
+        for run in range(4):
+            at = (j * 4 + run) * C
+            image_out[:, (run * 4 + j) * C : (run * 4 + j + 1) * C] = grad[:, at : at + C]
+
+    for copy in z_back:
         copy.wait_recv()
     for copy in copies:
         copy.wait_send()
@@ -344,17 +369,23 @@
     vmem = pl.BlockSpec(memory_space=pltpu.VMEM)
     smem = pl.BlockSpec(memory_space=pltpu.SMEM)
     block = (W, D)
-    return pl.pallas_call(
+    text_grad, image_grad = pl.pallas_call(
         kernel,
         out_shape=(
-            jax.ShapeDtypeStruct((NT * W, C), F32),
+            jax.ShapeDtypeStruct((C, NT * W), F32),
             jax.ShapeDtypeStruct(block, F32),
         ),
-        in_specs=[anywhere, anywhere, vmem, smem, smem],
+        in_specs=[anywhere, anywhere, anywhere, smem, smem],
         out_specs=(vmem, vmem),
         scratch_shapes=[
-            pltpu.VMEM((NT, W, C), BF16),
-            pltpu.VMEM((NT, W, C), BF16),
+            pltpu.VMEM((C, NT * W), BF16),
+            pltpu.VMEM((C, NT * W), BF16),
+            pltpu.VMEM((128, 128), jnp.int32),
+            pltpu.VMEM((4, 2, C + 8, 128), BF16),
+            pltpu.VMEM((4, 2, C + 8, 128), BF16),
+            pltpu.VMEM((384, 128), F32),
+            pltpu.VMEM((4, 2, W, 384), BF16),
+            pltpu.VMEM((4, 2, W, 384), BF16),
             pltpu.VMEM(block, F32),
             pltpu.VMEM(block, F32),
             pltpu.VMEM(block, F32),
@@ -375,15 +406,18 @@
             pltpu.VMEM((4, 4) + block, BF16),
             pltpu.VMEM((4,) + block, BF16),
             pltpu.VMEM((4,) + block, BF16),
-            pltpu.VMEM((NT, W, C), F32),
+            pltpu.VMEM((4, W, 384), F32),
+            pltpu.VMEM((4, W, 384), F32),
+            pltpu.VMEM((4, C, 128), F32),
             pltpu.SemaphoreType.DMA((COPIES,)),
             pltpu.SemaphoreType.DMA((COPIES,)),
-            pltpu.SemaphoreType.DMA((2,)),
+            pltpu.SemaphoreType.DMA((3,)),
         ],
         compiler_params=pltpu.CompilerParams(
             collective_id=0, has_side_effects=True, vmem_limit_bytes=50 * 2**20
         ),
-    )(text_feats, image_feats, group_ids.reshape(128, 128), log_scale, bias)
+    )(text_feats.T, image_feats.T, group_ids.reshape(128, 128), log_scale, bias)
+    return (text_grad.T, image_grad)
 
 
 def solution(mesh):

time: 85.4 us -> 85.2 us (level); the launches traced: 85.2 us -> 83.7 us
  Pallas kernels: 79.9 us -> 77.9 us
    pallas_call x1, Pallas kernels: 79.9 us -> 77.9 us  [body(): pl.pallas_call(kernel, out_shape=(jax.ShapeDtypeStruct((C, NT * W), F32),...]
    unnamed x7 -> x8, local copies, waits for them, and re-layouts: 2.53 us -> 3.92 us
where the time goes in v3:
time: 85.2 us; the launch traced here: 83.7 us
  Pallas kernels  77.9 us (91%)
  local copies, waits for them, and re-layouts  3.92 us (5%)
  between operations  1.94 us (2%)
    pallas_call x1, Pallas kernels, body(): pl.pallas_call(kernel, out_shape=(jax.ShapeDtypeStruct((C, NT * W), F32),...  77.9 us
    unnamed x8, local copies, waits for them, and re-layouts  3.92 us

profile of v3, /device:TPU:6, one launch (start us, length us, event | category | flops | bytes accessed | tf_op | source)
XLA Modules:
  0.0 83.7 jit_solution(3107384788561869809)
XLA Ops:
  1.9 0.0 copy-start
  1.9 0.9 %copy-done = bf16[512,72]{0,1:T(8,128)(2,1)S(1)} copy-done((bf16[512,72]{0,1:T(8,128)(2,1)S(1)}, bf16[512,72]{0,1:T(8,128)(2,1)}, u32[]{:S(2)}) %copy-start) | copy-done | bytes 73752
  2.8 0.0 copy-start.1
  2.8 0.9 %copy-done.1 = bf16[512,72]{0,1:T(8,128)(2,1)S(1)} copy-done((bf16[512,72]{0,1:T(8,128)(2,1)S(1)}, bf16[512,72]{0,1:T(8,128)(2,1)}, u32[]{:S(2)}) %copy-start.1) | copy-done | bytes 73752
  3.7 0.0 copy-start.2
  3.7 0.8 copy-done.2
  4.5 77.9 %shard_map.68 = (f32[72,512]{1,0:T(8,128)S(1)}, f32[32,1152]{1,0:T(8,128)S(1)}) custom-call(bf16[72,512]{1,0:T(8,128)(2,1)S(1)} %bitcast.5, bf16[72,512]{1,0:T(8,128)(2,1)S(1)} %bitcast.6, s32[128,128]{1,0:T(8,128)S(1)} %bitcast.7, f32[1]{0:T(128)S(6)} %copy.9.log_scale_ref, f32[1]{0:T(128)S(6)} %copy.10.bias_ref), custom_call_target="tpu_custom_call" | custom-call | tf_op jit(solution)/shard_map/pallas_call | solution.py:372
  82.4 0.7 copy.11
  83.1 0.7 copy.12
Async XLA Ops:
  1.9 0.9 %copy-start = (bf16[512,72]{0,1:T(8,128)(2,1)S(1)}, bf16[512,72]{0,1:T(8,128)(2,1)}, u32[]{:S(2)}) copy-start(bf16[512,72]{0,1:T(8,128)(2,1)} %param.5) | copy-start | bytes 221188
  2.8 0.9 %copy-start.1 = (bf16[512,72]{0,1:T(8,128)(2,1)S(1)}, bf16[512,72]{0,1:T(8,128)(2,1)}, u32[]{:S(2)}) copy-start(bf16[512,72]{0,1:T(8,128)(2,1)} %param.6) | copy-start | bytes 221188
  3.7 0.8 %copy-start.2 = (s32[16384]{0:T(1024)S(1)}, s32[16384]{0:T(1024)}, u32[]{:S(2)}) copy-start(s32[16384]{0:T(1024)} %param.7) | copy-start | bytes 196612

commit v4 on v3

--- a/solution.py
+++ b/solution.py
@@ -13,7 +13,7 @@
 W = 32
 NT = 16
 C = D // NT
-COPIES = 160
+COPIES = 84
 
 PLACE = {0: 0, 1: 1, 7: 2, 2: 3, 6: 4, 3: 5, 5: 6, 4: 7}
 
@@ -82,12 +82,15 @@
     for kind, own in enumerate((text_own, image_own)):
         for run in range(4):
             piece = own[:, run * 128 : run * 128 + 128].astype(F32)
-            cols_out[run, kind] = jnp.concatenate([piece, jnp.zeros((8, 128), F32)], axis=0).astype(BF16)
+            cols_out[kind, run] = jnp.concatenate([piece, jnp.zeros((8, 128), F32)], axis=0).astype(BF16)
     pl.semaphore_wait(barrier, len(greeted))
-    run_pieces = [
-        remote(cols_out.at[(z_lo + k) % 4], cols_in.at[z_lo], z_run(k)) for k in (1, 3, 2)
-    ]
-    cols_in[z_lo] = cols_out[z_lo]
+    run_pieces = []
+    for kind in range(2):
+        run_pieces.append([
+            remote(cols_out.at[kind, (z_lo + k) % 4], cols_in.at[kind, z_lo], z_run(k))
+            for k in (1, 3, 2)
+        ])
+        cols_in[kind, z_lo] = cols_out[kind, z_lo]
 
     def id_row(y_at, z_at, core_at):
         at = (y_at * 4 + (z_at // 4) * 2 + core_at) * 4 + z_at % 4
@@ -117,24 +120,26 @@
     scale = jnp.exp(jnp.full((1, 128), log_scale_ref[0], F32))[:, :1]
     offset = bias_ref[0]
 
-    for copy in run_pieces:
-        copy.wait_recv()
+    turned[4 * C :, :] = jnp.zeros((384 - 4 * C, 128), F32)
+    x_pieces = []
     for kind in range(2):
+        for copy in run_pieces[kind]:
+            copy.wait_recv()
         for run in range(4):
-            turned[run * C : run * C + C, :] = cols_in[run, kind].astype(F32)[:C]
-        turned[4 * C :, :] = jnp.zeros((384 - 4 * C, 128), F32)
-        rows_out[:, kind] = turned[...].T.astype(BF16).reshape(4, W, 384)
-    x_pieces = [
-        remote(rows_out.at[(x + k) % 4], rows_in.at[x], along(dx=k)) for k in (1, 3, 2)
-    ]
-    rows_in[x] = rows_out[x]
-    for copy in x_pieces:
-        copy.wait_recv()
+            turned[run * C : run * C + C, :] = cols_in[kind, run].astype(F32)[:C]
+        rows_out[kind] = turned[...].T.astype(BF16).reshape(4, W, 384)
+        x_pieces.append([
+            remote(rows_out.at[kind, (x + k) % 4], rows_in.at[kind, x], along(dx=k))
+            for k in (1, 3, 2)
+        ])
+        rows_in[kind, x] = rows_out[kind, x]
 
     def normalize(kind, unit_ref):
+        for copy in x_pieces[kind]:
+            copy.wait_recv()
         total = jnp.zeros((W, 1), F32)
         for j in range(4):
-            wide = rows_in[j, kind].astype(F32)[:, : 4 * C]
+            wide = rows_in[kind, j].astype(F32)[:, : 4 * C]
             rows32[:, j * 4 * C : (j + 1) * 4 * C] = wide
             total = total + jnp.sum(wide * wide, axis=1, keepdims=True)
         inverse = lax.rsqrt(total + 1e-06)
@@ -260,8 +265,8 @@
             chain_out.at[number, hop], chain_in.at[number, hop], along(dy=1 if way == 0 else 7)
         )
 
-    for number in range(4):
-        chain_step(number, 0)
+    chain_step(0, 0)
+    chain_step(1, 0)
 
     def image_push(c, half):
         at = c * 512 + half * 256
@@ -295,21 +300,27 @@
         core_sums.append(
             remote(core_out.at[pl.ds(2 * half, 2)], core_in.at[pl.ds(2 * half, 2)], core_mate)
         )
+    chain_step(2, 0)
+    chain_step(3, 0)
     for half in (1, 0):
         image_sum[2 * half : 2 * half + 2] = image_push(0, half)
-    for number in range(4):
-        chain_step(number, 1)
     core_sums[0].wait_recv()
     x_send(2)
+    chain_step(0, 1)
+    chain_step(1, 1)
     x_send(3)
     core_sums[1].wait_recv()
     x_send(1)
+    chain_step(2, 1)
+    chain_step(3, 1)
     x_send(0)
-    for number in range(4):
-        chain_step(number, 2)
-    for number in range(2):
-        chain_step(number, 3)
+    chain_step(0, 2)
+    chain_step(1, 2)
+    chain_step(2, 2)
+    chain_step(3, 2)
     z_send(2)
+    chain_step(0, 3)
+    chain_step(1, 3)
     z_send(3)
 
     def gathered(p):
@@ -381,11 +392,11 @@
             pltpu.VMEM((C, NT * W), BF16),
             pltpu.VMEM((C, NT * W), BF16),
             pltpu.VMEM((128, 128), jnp.int32),
-            pltpu.VMEM((4, 2, C + 8, 128), BF16),
-            pltpu.VMEM((4, 2, C + 8, 128), BF16),
+            pltpu.VMEM((2, 4, C + 8, 128), BF16),
+            pltpu.VMEM((2, 4, C + 8, 128), BF16),
             pltpu.VMEM((384, 128), F32),
-            pltpu.VMEM((4, 2, W, 384), BF16),
-            pltpu.VMEM((4, 2, W, 384), BF16),
+            pltpu.VMEM((2, 4, W, 384), BF16),
+            pltpu.VMEM((2, 4, W, 384), BF16),
             pltpu.VMEM(block, F32),
             pltpu.VMEM(block, F32),
             pltpu.VMEM(block, F32),
@@ -414,7 +425,7 @@
             pltpu.SemaphoreType.DMA((3,)),
         ],
         compiler_params=pltpu.CompilerParams(
-            collective_id=0, has_side_effects=True, vmem_limit_bytes=50 * 2**20
+            collective_id=0, has_side_effects=True, vmem_limit_bytes=60 * 2**20
         ),
     )(text_feats.T, image_feats.T, group_ids.reshape(128, 128), log_scale, bias)
     return (text_grad.T, image_grad)

time: 85.2 us -> 79 us (0.927); the launches traced: 83.7 us -> 78.7 us
  Pallas kernels: 77.9 us -> 74.5 us
  local copies, waits for them, and re-layouts: 3.92 us -> 2.28 us
    pallas_call x1, Pallas kernels: 77.9 us -> 74.5 us  [body(): pl.pallas_call(kernel, out_shape=(jax.ShapeDtypeStruct((C, NT * W), F32),...]
    unnamed x8 -> x4, local copies, waits for them, and re-layouts: 3.92 us -> 2.28 us
where the time goes in v4:
time: 79 us; the launch traced here: 78.7 us
  Pallas kernels  74.5 us (94%)
  local copies, waits for them, and re-layouts  2.28 us (3%)
  between operations  1.94 us (2%)
    pallas_call x1, Pallas kernels, body(): pl.pallas_call(kernel, out_shape=(jax.ShapeDtypeStruct((C, NT * W), F32),...  74.5 us
    unnamed x4, local copies, waits for them, and re-layouts  2.28 us

profile of v4, /device:TPU:6, one launch (start us, length us, event | category | flops | bytes accessed | tf_op | source)
XLA Modules:
  0.0 78.7 jit_solution(14161986740191365978)
XLA Ops:
  1.9 74.5 %shard_map.68 = (f32[72,512]{1,0:T(8,128)}, f32[32,1152]{1,0:T(8,128)}) custom-call(bf16[72,512]{1,0:T(8,128)(2,1)} %bitcast.5, bf16[72,512]{1,0:T(8,128)(2,1)} %bitcast.6, s32[128,128]{1,0:T(8,128)} %bitcast.7, f32[1]{0:T(128)S(6)} %copy.9.log_scale_ref, f32[1]{0:T(128)S(6)} %copy.10.bias_ref), custom_call_target="tpu_custom_call" | custom-call | tf_op jit(solution)/shard_map/pallas_call | solution.py:383
  76.4 0.0 copy-start
  76.4 1.6 %copy.11 = f32[512,72]{0,1:T(8,128)} copy(f32[512,72]{0,1:T(8,128)} %bitcast.4) | data formatting | bytes 294912
  78.0 0.0 copy-done
  78.0 0.7 copy.12
Async XLA Ops:
  76.4 1.6 %copy-start = (f32[32,1152]{1,0:T(8,128)S(1)}, f32[32,1152]{1,0:T(8,128)}, u32[]{:S(2)}) copy-start(f32[32,1152]{1,0:T(8,128)} %get-tuple-element.9) | copy-start | bytes 442372

commit v5 on v4

--- a/solution.py
+++ b/solution.py
@@ -30,7 +30,7 @@
     txt, img, text_ids, image_ids, slopes,
     text_sum, chain_out, chain_in, pair_out, pair_in,
     image_sum, core_out, core_in, x_out, x_in, z_out, z_in,
-    grad_out, grad_in, back_out,
+    grad_out, grad_in, back_out, back_in,
     send_sem, recv_sem, local_sem,
 ):
     dp, tensor = lax.axis_index("dp"), lax.axis_index("tensor")
@@ -45,6 +45,9 @@
     z_lo = z % 4
     z_mate = device_at(y, z + 1 - 2 * parity, core, x)
     core_mate = along(flip=True)
+
+    def slant(dy):
+        return device_at((y + dy) % 8, z + 1 - 2 * parity, core, x)
 
     def z_run(k):
         return device_at(y, z - z_lo + (z_lo + k) % 4, core, x)
@@ -74,6 +77,7 @@
     greeted = [z_run(k) for k in (1, 2, 3)] + [along(dx=k) for k in (1, 2, 3)]
     greeted += [core_mate, along(dy=1), along(dy=7), along(dz=4)]
     greeted += [device_at(y, (z + 2 + 4 * (1 - z_lo // 2)) % 8, core, x)]
+    greeted += [slant(1), slant(7)]
     for device in greeted:
         pl.semaphore_signal(barrier, inc=1, device_id=device, device_id_type=MESH)
 
@@ -85,12 +89,15 @@
             cols_out[kind, run] = jnp.concatenate([piece, jnp.zeros((8, 128), F32)], axis=0).astype(BF16)
     pl.semaphore_wait(barrier, len(greeted))
     run_pieces = []
-    for kind in range(2):
+
+    def send_run(kind):
         run_pieces.append([
             remote(cols_out.at[kind, (z_lo + k) % 4], cols_in.at[kind, z_lo], z_run(k))
             for k in (1, 3, 2)
         ])
         cols_in[kind, z_lo] = cols_out[kind, z_lo]
+
+    send_run(0)
 
     def id_row(y_at, z_at, core_at):
         at = (y_at * 4 + (z_at // 4) * 2 + core_at) * 4 + z_at % 4
@@ -117,6 +124,7 @@
             at = (c * 4 + q) * 128
             image_ids[:, at : at + 128] = from_x
 
+    send_run(1)
     scale = jnp.exp(jnp.full((1, 128), log_scale_ref[0], F32))[:, :1]
     offset = bias_ref[0]
 
@@ -161,7 +169,6 @@
             arrive[r + 1] = remote(text_slot(r, p), text_slot(r + 1, p), along(dy=7))
         return arrive
 
-    pair = remote(text_slot(0, 0), text_slot(0, 1), z_mate)
     waiting = {(r, 0): copy for r, copy in forward(0, 0).items()}
 
     def text_step(r, p):
@@ -186,9 +193,10 @@
             x_wait.pop((q, k)).wait_recv()
         core_wait[q] = remote(img.at[0, q], img.at[1, q], core_mate)
 
+    waiting[(7, 1)] = remote(text_slot(0, 0), text_slot(7, 1), slant(1))
+    waiting[(1, 1)] = remote(text_slot(0, 0), text_slot(1, 1), slant(7))
+    pair = remote(text_slot(0, 0), text_slot(0, 1), z_mate)
     spread_x(0)
-    pair.wait_recv()
-    waiting.update({(s, 1): copy for s, copy in forward(0, 1).items()})
     text_step(7, 0)
     text_step(1, 0)
     for q in (1, 3):
@@ -196,6 +204,7 @@
         spread_x(q)
     text_step(7, 1)
     text_step(1, 1)
+    pair.wait_recv()
     z_wait[2].wait_recv()
     spread_x(2)
     text_step(6, 0)
@@ -239,6 +248,8 @@
         for half in range(2):
             tile(0, c, half)
     text_push(0)
+    pair_out[...] = text_sum[0, 1].astype(BF16)
+    mate_sum = remote(pair_out, pair_in, z_mate)
     text_step(4, 0)
     text_step(4, 1)
     for c in range(2):
@@ -261,9 +272,9 @@
             arrived[number].wait_recv()
             part = part + chain_in[number, hop - 1].astype(F32)
         chain_out[number, hop] = part.astype(BF16)
-        arrived[number] = remote(
-            chain_out.at[number, hop], chain_in.at[number, hop], along(dy=1 if way == 0 else 7)
-        )
+        dy = 1 if way == 0 else 7
+        device = slant(dy) if p == 1 and slots[hop] in (1, 7) else along(dy=dy)
+        arrived[number] = remote(chain_out.at[number, hop], chain_in.at[number, hop], device)
 
     chain_step(0, 0)
     chain_step(1, 0)
@@ -323,42 +334,36 @@
     chain_step(1, 3)
     z_send(3)
 
-    def gathered(p):
-        total = text_sum[0, p]
-        for number, (way, chain_p, slots) in enumerate(chains):
-            if chain_p == p:
-                arrived[number].wait_recv()
-                total = total + chain_in[number, len(slots) - 1].astype(F32)
-        return total
-
     def unit_back(push, unit, inverse):
         push = push * scale
         return (push - unit * jnp.sum(unit * push, axis=1, keepdims=True)) * inverse
 
-    pair_out[...] = gathered(1).astype(BF16)
-    mate_sum = remote(pair_out, pair_in, z_mate)
-    z_send(1)
-    push = gathered(0)
     mate_sum.wait_recv()
-    grad = unit_back(push + pair_in[...].astype(F32), text_unit[...], text_inverse)
+    push = text_sum[0, 0] + pair_in[...].astype(F32)
+    for number in (2, 3, 0, 1):
+        arrived[number].wait_recv()
+        push = push + chain_in[number, len(chains[number][2]) - 1].astype(F32)
+    grad = unit_back(push, text_unit[...], text_inverse)
     blank = jnp.zeros((W, 384 - 4 * C), F32)
     for j in range(4):
-        grad_out[j] = jnp.concatenate([grad[:, j * 4 * C : (j + 1) * 4 * C], blank], axis=1)
+        piece = grad[:, j * 4 * C : (j + 1) * 4 * C]
+        grad_out[j] = jnp.concatenate([piece, blank], axis=1).astype(BF16)
     x_back = [
         remote(grad_out.at[(x + k) % 4], grad_in.at[x], along(dx=k)) for k in (1, 3, 2)
     ]
     grad_in[x] = grad_out[x]
+    z_send(1)
     image_push_total = z_part(0)
     for copy in x_back:
         copy.wait_recv()
-    down = grad_in[...].reshape(128, 384).T
+    down = grad_in[...].astype(F32).reshape(128, 384).T
     for run in range(4):
-        back_out[run] = down[run * C : run * C + C]
-    lanes = pl.ds(pl.multiple_of(z_lo * 128, 128), 128)
+        piece = down[run * C : run * C + C]
+        back_out[run] = jnp.concatenate([piece, jnp.zeros((8, 128), F32)], axis=0).astype(BF16)
     z_back = [
-        remote(back_out.at[(z_lo + k) % 4], text_out.at[:, lanes], z_run(k)) for k in (1, 3, 2)
+        remote(back_out.at[(z_lo + k) % 4], back_in.at[z_lo], z_run(k)) for k in (1, 3, 2)
     ]
-    text_out[:, lanes] = back_out[z_lo]
+    back_in[z_lo] = back_out[z_lo]
 
     for q in (1, 3, 2):
         z_sums[q].wait_recv()
@@ -371,12 +376,14 @@
 
     for copy in z_back:
         copy.wait_recv()
+    for run in range(4):
+        text_out[:, run * 128 : run * 128 + 128] = back_in[run].astype(F32)[:C]
     for copy in copies:
         copy.wait_send()
 
 
 def body(text_feats, image_feats, group_ids, log_scale, bias):
-    anywhere = pl.BlockSpec(memory_space=pl.ANY)
+    hbm = pl.BlockSpec(memory_space=pltpu.HBM)
     vmem = pl.BlockSpec(memory_space=pltpu.VMEM)
     smem = pl.BlockSpec(memory_space=pltpu.SMEM)
     block = (W, D)
@@ -386,7 +393,7 @@
             jax.ShapeDtypeStruct((C, NT * W), F32),
             jax.ShapeDtypeStruct(block, F32),
         ),
-        in_specs=[anywhere, anywhere, anywhere, smem, smem],
+        in_specs=[hbm, hbm, hbm, smem, smem],
         out_specs=(vmem, vmem),
         scratch_shapes=[
             pltpu.VMEM((C, NT * W), BF16),
@@ -417,9 +424,10 @@
             pltpu.VMEM((4, 4) + block, BF16),
             pltpu.VMEM((4,) + block, BF16),
             pltpu.VMEM((4,) + block, BF16),
-            pltpu.VMEM((4, W, 384), F32),
-            pltpu.VMEM((4, W, 384), F32),
-            pltpu.VMEM((4, C, 128), F32),
+            pltpu.VMEM((4, W, 384), BF16),
+            pltpu.VMEM((4, W, 384), BF16),
+            pltpu.VMEM((4, C + 8, 128), BF16),
+            pltpu.VMEM((4, C + 8, 128), BF16),
             pltpu.SemaphoreType.DMA((COPIES,)),
             pltpu.SemaphoreType.DMA((COPIES,)),
             pltpu.SemaphoreType.DMA((3,)),

time: 79 us -> 77.2 us (0.977)
  the two profiles are of different devices: /device:TPU:6 before, /device:TPU:8 now
where the time goes in v5:
time: 77.2 us; the launch traced here: 77 us
  Pallas kernels  72.8 us (94%)
  local copies, waits for them, and re-layouts  2.28 us (3%)
  between operations  1.94 us (3%)
    pallas_call x1, Pallas kernels, body(): pl.pallas_call(kernel, out_shape=(jax.ShapeDtypeStruct((C, NT * W), F32),...  72.8 us
    unnamed x4, local copies, waits for them, and re-layouts  2.28 us

profile of v5, /device:TPU:8, one launch (start us, length us, event | category | flops | bytes accessed | tf_op | source)
XLA Modules:
  0.0 77.0 jit_solution(15828470730275718760)
XLA Ops:
  1.9 72.8 %shard_map.68 = (f32[72,512]{1,0:T(8,128)}, f32[32,1152]{1,0:T(8,128)}) custom-call(bf16[72,512]{1,0:T(8,128)(2,1)} %bitcast.5, bf16[72,512]{1,0:T(8,128)(2,1)} %bitcast.6, s32[128,128]{1,0:T(8,128)} %bitcast.7, f32[1]{0:T(128)S(6)} %copy.9.log_scale_ref, f32[1]{0:T(128)S(6)} %copy.10.bias_ref), custom_call_target="tpu_custom_call" | custom-call | tf_op jit(solution)/shard_map/pallas_call | solution.py:390
  74.7 0.0 copy-start
  74.8 1.6 %copy.11 = f32[512,72]{0,1:T(8,128)} copy(f32[512,72]{0,1:T(8,128)} %bitcast.4) | data formatting | bytes 294912
  76.4 0.0 copy-done
  76.4 0.7 copy.12
Async XLA Ops:
  74.7 1.6 %copy-start = (f32[32,1152]{1,0:T(8,128)S(1)}, f32[32,1152]{1,0:T(8,128)}, u32[]{:S(2)}) copy-start(f32[32,1152]{1,0:T(8,128)} %get-tuple-element.9) | copy-start | bytes 442372

commit v6 on v5

--- a/solution.py
+++ b/solution.py
@@ -220,6 +220,8 @@
     text_step(3, 0)
     to_core(2)
 
+    gather_copies = len(copies)
+
     def tile(batch, c, half):
         rows = txt[4 * batch : 4 * batch + 4].reshape(256, D)
         cols = img[c, 2 * half : 2 * half + 2].reshape(256, D)
@@ -315,6 +317,8 @@
     chain_step(3, 0)
     for half in (1, 0):
         image_sum[2 * half : 2 * half + 2] = image_push(0, half)
+    for copy in copies[:gather_copies]:
+        copy.wait_send()
     core_sums[0].wait_recv()
     x_send(2)
     chain_step(0, 1)
@@ -374,12 +378,12 @@
             at = (j * 4 + run) * C
             image_out[:, (run * 4 + j) * C : (run * 4 + j + 1) * C] = grad[:, at : at + C]
 
+    for copy in copies[gather_copies:]:
+        copy.wait_send()
     for copy in z_back:
         copy.wait_recv()
     for run in range(4):
         text_out[:, run * 128 : run * 128 + 128] = back_in[run].astype(F32)[:C]
-    for copy in copies:
-        copy.wait_send()
 
 
 def body(text_feats, image_feats, group_ids, log_scale, bias):

time: 77.2 us -> 77.1 us (level)
  no operation moved by 1% of the time
where the time goes in v6:
time: 77.1 us; the launch traced here: 76.9 us
  Pallas kernels  72.7 us (94%)
  local copies, waits for them, and re-layouts  2.28 us (3%)
  between operations  1.94 us (3%)
    pallas_call x1, Pallas kernels, body(): pl.pallas_call(kernel, out_shape=(jax.ShapeDtypeStruct((C, NT * W), F32),...  72.7 us
    unnamed x4, local copies, waits for them, and re-layouts  2.28 us

profile of v6, /device:TPU:8, one launch (start us, length us, event | category | flops | bytes accessed | tf_op | source)
XLA Modules:
  0.0 76.9 jit_solution(2169253885480025659)
XLA Ops:
  1.9 72.7 %shard_map.68 = (f32[72,512]{1,0:T(8,128)}, f32[32,1152]{1,0:T(8,128)}) custom-call(bf16[72,512]{1,0:T(8,128)(2,1)} %bitcast.5, bf16[72,512]{1,0:T(8,128)(2,1)} %bitcast.6, s32[128,128]{1,0:T(8,128)} %bitcast.7, f32[1]{0:T(128)S(6)} %copy.9.log_scale_ref, f32[1]{0:T(128)S(6)} %copy.10.bias_ref), custom_call_target="tpu_custom_call" | custom-call | tf_op jit(solution)/shard_map/pallas_call | solution.py:394
  74.6 0.0 copy-start
  74.6 1.6 %copy.11 = f32[512,72]{0,1:T(8,128)} copy(f32[512,72]{0,1:T(8,128)} %bitcast.4) | data formatting | bytes 294912
  76.2 0.0 copy-done
  76.2 0.7 copy.12
Async XLA Ops:
  74.6 1.6 %copy-start = (f32[32,1152]{1,0:T(8,128)S(1)}, f32[32,1152]{1,0:T(8,128)}, u32[]{:S(2)}) copy-start(f32[32,1152]{1,0:T(8,128)} %get-tuple-element.9) | copy-start | bytes 442372
